TPU v7x, 32 devices: a whole 2x2x4 slice. The times are simulated.
32 devices in a mesh: query: 4 (over x, core), bank: 8 (over z, y).
Axes of the slice: x: 2, y: 2, z: 4, core: 2. Of those that a mesh axis runs over, the one named last changes fastest.
Arguments:
- queries: bfloat16 [256, 32, 128], P(('query', 'bank'))
- passages: bfloat16 [2048, 128, 128], P('bank')
- passage_home: int32 [2048], replicated, may hold values from 0 to 2047, as said below
- candidates: int32 [256, 16], P(('query', 'bank')), may hold values from 0 to 2047, as said below
- positive: int32 [256], P(('query', 'bank')), may hold values from 0 to 15
Outputs:
- losses: float32 [256], P(('query', 'bank'))
- query_grads: float32 [256, 32, 128], P(('query', 'bank'))
Inputs may be any that keep to these rules, and one draw needn't show every extreme that they name: `passage_home`: each passage id has its own storage row; storage row r lies on bank index r // 256. `candidates`: among the 128 list entries of one device's queries (aligned blocks of 8 queries, in order), at most 48 name passages stored on one bank index; in every block some bank index gets exactly 48, and in each group of 8 consecutive blocks it is the same bank index for all of them.
All inputs are finite; a program needn't handle non-finite values.
Results may differ from a plain program's by a relative error of at most 0.0049.
Values may be sent and summed in bfloat16 or wider, within the bound.
A program may use at most 128 MiB of HBM per device.

v0:
```python
import functools

import jax
import jax.numpy as jnp
from jax import lax
from jax.experimental import pallas as pl
from jax.experimental.pallas import tpu as pltpu
from jax.sharding import PartitionSpec as P

GROUP = 48


MESH = pl.DeviceIdType.MESH


def quarter_sum(x):
    n = x.shape[0] // 4
    return (x[:n] + x[n : 2 * n]) + (x[2 * n : 3 * n] + x[3 * n :])


def quarter_product(x):
    n = x.shape[0] // 4
    return (x[:n] * x[n : 2 * n]) * (x[2 * n : 3 * n] * x[3 * n :])


def pair_kernel(row_ref, qid_ref, queries_ref, passages_ref, basis_ref, sim_ref, held, arrived):
    groups = row_ref.shape[0] // GROUP
    query_len, feature_dim = queries_ref.shape[1:]
    length = held.shape[2]

    def fetch(group, u):
        half = lax.rem(group, 2)
        return pltpu.make_async_copy(
            passages_ref.at[row_ref[group * GROUP + u]], held.at[half, u], arrived.at[half, u]
        )

    for u in range(GROUP):
        fetch(0, u).start()

    @pl.loop(0, groups)
    def _(group):
        first = group * GROUP

        @pl.when(group + 1 < groups)
        def _():
            for u in range(GROUP):
                fetch(group + 1, u).start()

        for u in range(GROUP):
            fetch(group, u).wait()
        half = lax.rem(group, 2)
        pairs, scores = [], []
        for u in range(0, GROUP, 2):
            tile = held[half, u : u + 2].reshape(2 * length, feature_dim)
            stacked = jnp.concatenate(
                [queries_ref[qid_ref[first + u]], queries_ref[qid_ref[first + u + 1]]], axis=0
            )
            both = lax.dot_general(
                stacked, tile, (((1,), (1,)), ((), ())), preferred_element_type=jnp.float32
            )
            pairs.append(tile)
            scores += [both[:query_len, :length], both[query_len:, length:]]
        largest = [jnp.max(s, axis=1, keepdims=True) for s in scores]
        raised = [jnp.exp(s - m) for s, m in zip(scores, largest)]
        totals = [jnp.sum(r, axis=1, keepdims=True) for r in raised]
        guesses = [pl.reciprocal(t, approx=True) for t in totals]
        inverse = [g * (2.0 - t * g) for g, t in zip(guesses, totals)]
        weights = [(r * v).astype(jnp.bfloat16) for r, v in zip(raised, inverse)]
        blank = jnp.zeros((query_len, length), jnp.bfloat16)
        for u in range(0, GROUP, 2):
            spread = jnp.concatenate(
                [
                    jnp.concatenate([weights[u], blank], axis=1),
                    jnp.concatenate([blank, weights[u + 1]], axis=1),
                ],
                axis=0,
            )
            both = jnp.dot(spread, pairs[u // 2], preferred_element_type=jnp.float32)
            basis_ref[first + u] = both[:query_len].astype(jnp.bfloat16)
            basis_ref[first + u + 1] = both[query_len:].astype(jnp.bfloat16)
        rows = [
            jnp.sum(quarter_sum(m) + jnp.log(quarter_product(t)), axis=0, keepdims=True)
            for m, t in zip(largest, totals)
        ]
        sim_ref[pl.ds(pl.multiple_of(first, GROUP), GROUP), :] = jnp.broadcast_to(
            jnp.concatenate(rows, axis=0), (GROUP, sim_ref.shape[1])
        )


def pair_terms(rows, qids, queries, passages):
    slots = rows.shape[0]
    query_len, feature_dim = queries.shape[1:]
    return pl.pallas_call(
        pair_kernel,
        out_shape=(
            jax.ShapeDtypeStruct((slots, query_len, feature_dim), jnp.bfloat16),
            jax.ShapeDtypeStruct((slots, 128), jnp.float32),
        ),
        in_specs=[pl.BlockSpec(memory_space=pltpu.SMEM)] * 2
        + [pl.BlockSpec(memory_space=pltpu.VMEM), pl.BlockSpec(memory_space=pltpu.HBM)],
        out_specs=(pl.BlockSpec(memory_space=pltpu.VMEM),) * 2,
        scratch_shapes=[
            pltpu.VMEM((2, GROUP) + passages.shape[1:], passages.dtype),
            pltpu.SemaphoreType.DMA((2, GROUP)),
        ],
        compiler_params=pltpu.CompilerParams(vmem_limit_bytes=48 * 1024 * 1024),
    )(rows, qids, queries, passages)


def greet(shards, me):
    barrier = pltpu.get_barrier_semaphore()
    for step in range(1, shards):
        pl.semaphore_signal(
            barrier, inc=1, device_id={"bank": lax.rem(me + step, shards)}, device_id_type=MESH
        )
    pl.semaphore_wait(barrier, shards - 1)


def gather_kernel(shards, inner, q_ref, info_ref, all_q_ref, all_info_ref, sends, recvs, isends, irecvs):
    outer = shards // inner
    me = lax.axis_index("bank")
    z, y = me // inner, lax.rem(me, inner)
    rows = q_ref.shape[0]

    def place(index):
        return pl.ds(pl.multiple_of(index * rows, rows), rows)

    def peer(dz, dy):
        return lax.rem(z + dz, outer) * inner + lax.rem(y + dy, inner)

    def send(src, block, slot, target):
        copy = pltpu.make_async_remote_copy(
            src_ref=src,
            dst_ref=all_q_ref.at[place(block)],
            send_sem=sends.at[slot],
            recv_sem=recvs.at[slot],
            device_id={"bank": target},
            device_id_type=MESH,
        )
        copy.start()
        return copy

    greet(shards, me)
    copies = {}
    for dz in range(1, outer):
        copies[dz * inner] = send(q_ref, me, dz * inner, peer(dz, 0))
    small = []
    for step in range(1, shards):
        copy = pltpu.make_async_remote_copy(
            src_ref=info_ref,
            dst_ref=all_info_ref.at[place(me)],
            send_sem=isends.at[step],
            recv_sem=irecvs.at[step],
            device_id={"bank": lax.rem(me + step, shards)},
            device_id_type=MESH,
        )
        copy.start()
        small.append(copy)
    for dy in range(1, inner):
        copies[dy] = send(q_ref, me, dy, peer(0, dy))
    all_q_ref[place(me)] = q_ref[...]
    all_info_ref[place(me)] = info_ref[...]
    for dz in range(1, outer):
        copies[dz * inner].wait_recv()
        source = lax.rem(z + outer - dz, outer) * inner + y
        for dy in range(1, inner):
            copies[dz * inner + dy] = send(
                all_q_ref.at[place(source)], source, dz * inner + dy, peer(0, dy)
            )
    for slot, copy in copies.items():
        if slot < inner or slot % inner:
            copy.wait_recv()
        copy.wait_send()
    for copy in small:
        copy.wait()


def gather_queries(queries, info):
    shards = lax.axis_size("bank")
    inner = 1
    while (2 * inner) ** 2 <= shards:
        inner *= 2
    vmem = pl.BlockSpec(memory_space=pltpu.VMEM)
    return pl.pallas_call(
        functools.partial(gather_kernel, shards, inner),
        out_shape=(
            jax.ShapeDtypeStruct((shards * queries.shape[0],) + queries.shape[1:], queries.dtype),
            jax.ShapeDtypeStruct((shards * info.shape[0], info.shape[1]), info.dtype),
        ),
        in_specs=[vmem, vmem],
        out_specs=(vmem, vmem),
        scratch_shapes=[pltpu.SemaphoreType.DMA((shards,))] * 4,
        compiler_params=pltpu.CompilerParams(
            collective_id=0, has_side_effects=True, vmem_limit_bytes=16 * 1024 * 1024
        ),
    )(queries, info)


def contrast_kernel(shards, sim_ref, meta_ref, coef_ref, loss_ref, slots, sends, recvs):
    me = lax.axis_index("bank")
    width = coef_ref.shape[1]
    capacity = sim_ref.shape[0]
    meta = meta_ref[...]
    lane = lax.broadcasted_iota(jnp.int32, (capacity, width), 1)
    chosen = meta == lane * 2 + 1
    match = chosen | (meta == lane * 2)
    table = jnp.where(match, sim_ref[:, :1], -jnp.inf)
    largest = jnp.max(table, axis=0, keepdims=True)
    safe = jnp.where(largest == -jnp.inf, 0.0, largest)
    partial = jnp.sum(jnp.exp(table - safe), axis=0, keepdims=True)
    wanted = jnp.sum(jnp.where(chosen, table, 0.0), axis=0, keepdims=True)
    slots[me] = jnp.concatenate([largest, partial, wanted, jnp.zeros((5, width), jnp.float32)], axis=0)
    greet(shards, me)
    copies = []
    for step in range(1, shards):
        copy = pltpu.make_async_remote_copy(
            src_ref=slots.at[me],
            dst_ref=slots.at[me],
            send_sem=sends.at[step],
            recv_sem=recvs.at[step],
            device_id={"bank": lax.rem(me + step, shards)},
            device_id_type=MESH,
        )
        copy.start()
        copies.append(copy)
    for copy in copies:
        copy.wait()
    tops = [slots[b, 0:1, :] for b in range(shards)]
    top = functools.reduce(jnp.maximum, tops)
    top = jnp.where(top == -jnp.inf, 0.0, top)
    total = sum(slots[b, 1:2, :] * jnp.exp(tops[b] - top) for b in range(shards))
    picked = sum(slots[b, 2:3, :] for b in range(shards))
    loss_ref[...] = jnp.broadcast_to(top + jnp.log(total) - picked, loss_ref.shape)
    total = jnp.where(total == 0.0, 1.0, total)
    shares = jnp.exp(table - top) / total
    coef_ref[...] = (shares - jnp.where(chosen, 1.0, 0.0)).astype(coef_ref.dtype)


def contrast(sims, meta, group):
    shards = lax.axis_size("bank")
    width = -(-group // 128) * 128
    vmem = pl.BlockSpec(memory_space=pltpu.VMEM)
    return pl.pallas_call(
        functools.partial(contrast_kernel, shards),
        out_shape=(
            jax.ShapeDtypeStruct((sims.shape[0], width), jnp.bfloat16),
            jax.ShapeDtypeStruct((8, width), jnp.float32),
        ),
        in_specs=[vmem, vmem],
        out_specs=(vmem, vmem),
        scratch_shapes=[
            pltpu.VMEM((shards, 8, width), jnp.float32),
            pltpu.SemaphoreType.DMA((shards,)),
            pltpu.SemaphoreType.DMA((shards,)),
        ],
        compiler_params=pltpu.CompilerParams(
            collective_id=1, has_side_effects=True, vmem_limit_bytes=16 * 1024 * 1024
        ),
    )(sims, meta)


def slot_list(storage, positive, holdings, capacity):
    count, listed = storage.shape
    me = lax.axis_index("bank")
    owned = (storage // holdings == me).reshape(-1)
    entry = jnp.arange(count * listed, dtype=jnp.int32)
    picked = (jnp.arange(listed, dtype=jnp.int32)[None, :] == positive[:, None]).astype(jnp.int32)
    query = entry // listed
    code = (query * 2 + picked.reshape(-1)) * holdings + (storage % holdings).reshape(-1)
    position = jnp.cumsum(owned.astype(jnp.int32)) - 1
    target = jnp.where(owned, position, -1)
    here = target[None, :] == jnp.arange(capacity, dtype=jnp.int32)[:, None]
    table = jnp.sum(jnp.where(here, code[None, :] + 1, 0), axis=1) - 1
    meta = jnp.where(table >= 0, table // holdings, -1)
    table = jnp.maximum(table, 0)
    return table % holdings, table // holdings // 2, meta


def body(queries, passages, passage_home, candidates, positive):
    shards = lax.axis_size("bank")
    query_rows, query_len, feature_dim = queries.shape
    listed = candidates.shape[1]
    holdings = passages.shape[0]
    capacity = 3 * query_rows * listed
    group = shards * query_rows
    info = jnp.concatenate([passage_home[candidates], positive[:, None]], axis=1)
    info = jnp.pad(info, ((0, 0), (0, 128 - info.shape[1])))
    all_queries, infos = gather_queries(queries, info)
    rows, qids, meta = slot_list(infos[:, :listed], infos[:, listed], holdings, capacity)
    basis, sims = pair_terms(rows, qids, all_queries, passages)
    coefficients, losses = contrast(sims, meta[:, None], group)
    mine = lax.axis_index("bank") * query_rows
    losses = lax.dynamic_slice_in_dim(losses[0], mine, query_rows, 0)
    part = lax.dot_general(
        coefficients[:, :group],
        basis.reshape(capacity, query_len * feature_dim),
        (((0,), (0,)), ((), ())),
        preferred_element_type=jnp.float32,
    ).astype(jnp.bfloat16)
    parts = lax.all_to_all(
        part.reshape(shards, query_rows, query_len * feature_dim), "bank", 0, 0, tiled=True
    )
    gradient = jnp.sum(parts.astype(jnp.float32), axis=0)
    return (losses, gradient.reshape(query_rows, query_len, feature_dim))


def solution(mesh):
    return jax.shard_map(
        body,
        mesh=mesh,
        in_specs=(
            P(("query", "bank"), None, None),
            P("bank", None, None),
            P(),
            P(("query", "bank"), None),
            P(("query", "bank")),
        ),
        out_specs=(P(("query", "bank")), P(("query", "bank"), None, None)),
        check_vma=False,
    )
```

profile of v0, /device:TPU:0, one launch (start us, length us, event | category | flops | bytes accessed | tf_op | source)
XLA Modules:
  0.0 63.3 jit_solution(4283585631742600749)
XLA Ops:
  0.6 0.0 copy-start
  0.6 0.0 copy-start.2
  0.7 0.0 copy-start.1
  0.7 0.7 %compare_select_fusion = s32[8,16]{1,0:T(8,128)S(1)} fusion(s32[8,16]{1,0:T(8,128)} %param.8), kind=kLoop, calls=%fused_computation.37 | loop fusion | flops 384 | bytes 1024 | tf_op jit(solution)/shard_map/select_n | solution.py:286
  1.4 0.1 reshape.161
  1.5 0.0 copy-done
  1.5 1.1 %gather_fusion = s32[128]{0:T(128)S(1)} fusion(s32[2048]{0:T(1024)S(1)} %copy-done, s32[1024]{0:T(1024)S(1)} %pad_clamp_fusion), kind=kCustom, calls=%fused_computation | custom fusion | bytes 1536 | tf_op jit(solution)/shard_map/gather | solution.py:286
  2.6 0.1 reshape.160
  2.7 0.0 copy-done.2
  2.7 0.1 copy.14
  2.8 0.1 pad_add_fusion
  2.9 0.0 copy-done.1
  2.9 15.9 %shard_map.68 = (bf16[64,32,128]{2,1,0:T(8,128)(2,1)S(1)}, s32[64,128]{1,0:T(8,128)S(1)}) custom-call(bf16[8,32,128]{2,1,0:T(8,128)(2,1)S(1)} %copy-done.1, s32[8,128]{1,0:T(8,128)S(1)} %pad.4.info_ref), custom_call_target="tpu_custom_call" | custom-call | tf_op jit(solution)/shard_map/pallas_call | solution.py:184
  18.8 0.2 slice_reduce_fusion
  19.1 0.1 reshape.153
  19.2 0.1 reshape.157
  19.2 0.3 reduce-window.9
  19.5 0.1 slice.20
  19.6 0.1 slice_reduce_fusion.1
  19.7 0.1 reshape.151
  19.8 0.1 fusion.14
  19.9 0.1 reshape.158
  20.0 0.1 fusion.20
  20.1 0.2 select_reduce_fusion
  20.3 0.2 fusion.7.meta_ref
  20.5 16.3 %shard_map.69 = (bf16[384,32,128]{2,1,0:T(8,128)(2,1)S(1)}, f32[384,128]{1,0:T(8,128)S(1)}) custom-call(s32[384]{0:T(512)S(1)} %get-tuple-element.18.row_ref, s32[384]{0:T(512)S(1)} %get-tuple-element.19.qid_ref, bf16[64,32,128]{2,1,0:T(8,128)(2,1)S(1)} %get-tuple-element.9.queries_ref, bf16[256,128,128]{2,1,0:T(8,128)(2,1)} %passages_ref.1), custom_call_target="tpu_custom_call" | custom-call | tf_op jit(solution)/shard_map/pallas_call | solution.py:93
  36.9 7.2 %shard_map.70 = (bf16[384,128]{1,0:T(8,128)(2,1)S(1)}, f32[8,128]{1,0:T(8,128)S(1)}) custom-call(f32[384,128]{1,0:T(8,128)S(1)} %get-tuple-element.10.sim_ref, s32[384,1]{1,0:T(8,128)S(1)} %fusion.7.meta_ref), custom_call_target="tpu_custom_call" | custom-call | tf_op jit(solution)/shard_map/pallas_call | solution.py:243
  44.1 1.9 %fusion = bf16[8,8,4096]{2,1,0:T(8,128)(2,1)} fusion(bf16[48,8,32,128]{3,2,1,0:T(8,128)(2,1)S(1)} %bitcast.15, bf16[384,128]{1,0:T(8,128)(2,1)S(1)} %get-tuple-element.12), kind=kOutput, calls=%fused_computation.2 | convolution fusion | flops 201588736 | bytes 3768320 | tf_op jit(solution)/shard_map/dot_general | solution.py:294
  46.1 5.3 %all-to-all-start = ((bf16[8,8,4096]{2,1,0:T(8,128)(2,1)}), bf16[8,8,4096]{2,1,0:T(8,128)(2,1)S(1)}, u32[]{:S(2)}, u32[]{:S(2)}) async-start(bf16[8,8,4096]{2,1,0:T(8,128)(2,1)} %fusion), calls=%async_computation | async-start | bytes 1048576 | tf_op jit(solution)/shard_map/all_to_all | solution.py:300
  51.4 0.6 dynamic-slice_bitcast_fusion
  51.9 10.6 %all-to-all-done = bf16[8,8,4096]{2,1,0:T(8,128)(2,1)S(1)} async-done(((bf16[8,8,4096]{2,1,0:T(8,128)(2,1)}), bf16[8,8,4096]{2,1,0:T(8,128)(2,1)S(1)}, u32[]{:S(2)}, u32[]{:S(2)}) %all-to-all-start) | async-done | bytes 524320 | tf_op jit(solution)/shard_map/all_to_all | solution.py:300
  62.5 0.1 convert_reduce_fusion
  62.6 0.7 %copy.27 = f32[1,8,32,128]{3,2,1,0:T(8,128)} copy(f32[1,8,32,128]{3,1,2,0:T(8,128)S(1)} %bitcast.16) | data formatting | bytes 262144
  (7 shorter events, 0.1 us)
Async XLA Ops:
  0.6 0.9 %copy-start = (s32[2048]{0:T(1024)S(1)}, s32[2048]{0:T(1024)}, u32[]{:S(2)}) copy-start(s32[2048]{0:T(1024)} %param.7) | copy-start | bytes 24580
  0.6 2.1 %copy-start.2 = (s32[8]{0:T(128)S(1)}, s32[8]{0:T(128)}, u32[]{:S(2)}) copy-start(s32[8]{0:T(128)} %param.9) | copy-start | bytes 100
  0.7 2.2 %copy-start.1 = (bf16[8,32,128]{2,1,0:T(8,128)(2,1)S(1)}, bf16[8,32,128]{2,1,0:T(8,128)(2,1)}, u32[]{:S(2)}) copy-start(bf16[8,32,128]{2,1,0:T(8,128)(2,1)} %q_ref.1) | copy-start | bytes 196612
  46.1 16.4 %all-to-all-start = ((bf16[8,8,4096]{2,1,0:T(8,128)(2,1)}), bf16[8,8,4096]{2,1,0:T(8,128)(2,1)S(1)}, u32[]{:S(2)}, u32[]{:S(2)}) async-start(bf16[8,8,4096]{2,1,0:T(8,128)(2,1)} %fusion), calls=%async_computation | async-start | bytes 1048576 | tf_op jit(solution)/shard_map/all_to_all | solution.py:300
where the time goes:
time: 64.5 us; the launch traced here: 63.3 us
  Pallas kernels  39.5 us (61%)
  waiting for transfers between devices  10.6 us (16%)
  starting transfers between devices  5.27 us (8%)
  local copies, waits for them, and re-layouts  3.37 us (5%)
  matrix products  1.94 us (3%)
  other arithmetic  1.84 us (3%)
  between operations  0.75 us (1%)
    pallas_call x1, Pallas kernels, pair_terms(): pl.pallas_call(pair_kernel, out_shape=(jax.ShapeDtypeStruct((slots, query...  16.3 us
    pallas_call x1, Pallas kernels, gather_queries(): pl.pallas_call(functools.partial(gather_kernel, shards, inner), out_shape...  15.9 us
    all_to_all x1, waiting for transfers between devices, body(): lax.all_to_all(part.reshape(shards, query_rows, query_len * feature_dim),...  10.6 us
    pallas_call x1, Pallas kernels, contrast(): pl.pallas_call(functools.partial(contrast_kernel, shards), out_shape=(jax...  7.24 us
    all_to_all x1, starting transfers between devices, body(): lax.all_to_all(part.reshape(shards, query_rows, query_len * feature_dim),...  5.27 us
    dot_general x1, matrix products, body(): lax.dot_general(coefficients[:, :group], basis.reshape(capacity, query_le...  1.94 us
  transfers between devices with their start and end apart: 1, of which 1 were waited for; matrix products, arithmetic and copies ran while one was open for 1% of the time, Pallas kernels for 0%

commit v1 on v0

--- a/solution.py
+++ b/solution.py
@@ -7,7 +7,7 @@
 from jax.experimental.pallas import tpu as pltpu
 from jax.sharding import PartitionSpec as P
 
-GROUP = 48
+GROUP = 64
 
 
 MESH = pl.DeviceIdType.MESH

time: 64.5 us -> 63.8 us (0.989)
  no operation moved by 1% of the time
where the time goes in v1:
time: 63.8 us; the launch traced here: 62.9 us
  Pallas kernels  39.1 us (61%)
  waiting for transfers between devices  10.6 us (17%)
  starting transfers between devices  5.34 us (8%)
  local copies, waits for them, and re-layouts  3.37 us (5%)
  matrix products  1.94 us (3%)
  other arithmetic  1.84 us (3%)
  between operations  0.75 us (1%)
    pallas_call x1, Pallas kernels, pair_terms(): pl.pallas_call(pair_kernel, out_shape=(jax.ShapeDtypeStruct((slots, query...  16.1 us
    pallas_call x1, Pallas kernels, gather_queries(): pl.pallas_call(functools.partial(gather_kernel, shards, inner), out_shape...  15.9 us
    all_to_all x1, waiting for transfers between devices, body(): lax.all_to_all(part.reshape(shards, query_rows, query_len * feature_dim),...  10.6 us
    pallas_call x1, Pallas kernels, contrast(): pl.pallas_call(functools.partial(contrast_kernel, shards), out_shape=(jax...  7.02 us
    all_to_all x1, starting transfers between devices, body(): lax.all_to_all(part.reshape(shards, query_rows, query_len * feature_dim),...  5.34 us
    dot_general x1, matrix products, body(): lax.dot_general(coefficients[:, :group], basis.reshape(capacity, query_le...  1.94 us
  transfers between devices with their start and end apart: 1, of which 1 were waited for; matrix products, arithmetic and copies ran while one was open for 1% of the time, Pallas kernels for 0%

profile of v1, /device:TPU:0, one launch (start us, length us, event | category | flops | bytes accessed | tf_op | source)
XLA Modules:
  0.0 62.9 jit_solution(18203674443235915499)
XLA Ops:
  0.6 0.0 copy-start
  0.6 0.0 copy-start.2
  0.7 0.0 copy-start.1
  0.7 0.7 %compare_select_fusion = s32[8,16]{1,0:T(8,128)S(1)} fusion(s32[8,16]{1,0:T(8,128)} %param.8), kind=kLoop, calls=%fused_computation.37 | loop fusion | flops 384 | bytes 1024 | tf_op jit(solution)/shard_map/select_n | solution.py:286
  1.4 0.1 reshape.161
  1.5 0.0 copy-done
  1.5 1.1 %gather_fusion = s32[128]{0:T(128)S(1)} fusion(s32[2048]{0:T(1024)S(1)} %copy-done, s32[1024]{0:T(1024)S(1)} %pad_clamp_fusion), kind=kCustom, calls=%fused_computation | custom fusion | bytes 1536 | tf_op jit(solution)/shard_map/gather | solution.py:286
  2.6 0.1 reshape.160
  2.7 0.0 copy-done.2
  2.7 0.1 copy.14
  2.8 0.1 pad_add_fusion
  2.9 0.0 copy-done.1
  2.9 15.9 %shard_map.68 = (bf16[64,32,128]{2,1,0:T(8,128)(2,1)S(1)}, s32[64,128]{1,0:T(8,128)S(1)}) custom-call(bf16[8,32,128]{2,1,0:T(8,128)(2,1)S(1)} %copy-done.1, s32[8,128]{1,0:T(8,128)S(1)} %pad.4.info_ref), custom_call_target="tpu_custom_call" | custom-call | tf_op jit(solution)/shard_map/pallas_call | solution.py:184
  18.8 0.2 slice_reduce_fusion
  19.1 0.1 reshape.153
  19.2 0.1 reshape.157
  19.2 0.3 reduce-window.9
  19.5 0.1 slice.20
  19.6 0.1 slice_reduce_fusion.1
  19.7 0.1 reshape.151
  19.8 0.1 fusion.14
  19.9 0.1 reshape.158
  20.0 0.1 fusion.20
  20.1 0.2 select_reduce_fusion
  20.3 0.2 fusion.7.meta_ref
  20.5 16.1 %shard_map.69 = (bf16[384,32,128]{2,1,0:T(8,128)(2,1)S(1)}, f32[384,128]{1,0:T(8,128)S(1)}) custom-call(s32[384]{0:T(512)S(1)} %get-tuple-element.18.row_ref, s32[384]{0:T(512)S(1)} %get-tuple-element.19.qid_ref, bf16[64,32,128]{2,1,0:T(8,128)(2,1)S(1)} %get-tuple-element.9.queries_ref, bf16[256,128,128]{2,1,0:T(8,128)(2,1)} %passages_ref.1), custom_call_target="tpu_custom_call" | custom-call | tf_op jit(solution)/shard_map/pallas_call | solution.py:93
  36.7 7.0 %shard_map.70 = (bf16[384,128]{1,0:T(8,128)(2,1)S(1)}, f32[8,128]{1,0:T(8,128)S(1)}) custom-call(f32[384,128]{1,0:T(8,128)S(1)} %get-tuple-element.10.sim_ref, s32[384,1]{1,0:T(8,128)S(1)} %fusion.7.meta_ref), custom_call_target="tpu_custom_call" | custom-call | tf_op jit(solution)/shard_map/pallas_call | solution.py:243
  43.7 1.9 %fusion = bf16[8,8,4096]{2,1,0:T(8,128)(2,1)} fusion(bf16[48,8,32,128]{3,2,1,0:T(8,128)(2,1)S(1)} %bitcast.15, bf16[384,128]{1,0:T(8,128)(2,1)S(1)} %get-tuple-element.12), kind=kOutput, calls=%fused_computation.2 | convolution fusion | flops 201588736 | bytes 3768320 | tf_op jit(solution)/shard_map/dot_general | solution.py:294
  45.6 5.3 %all-to-all-start = ((bf16[8,8,4096]{2,1,0:T(8,128)(2,1)}), bf16[8,8,4096]{2,1,0:T(8,128)(2,1)S(1)}, u32[]{:S(2)}, u32[]{:S(2)}) async-start(bf16[8,8,4096]{2,1,0:T(8,128)(2,1)} %fusion), calls=%async_computation | async-start | bytes 1048576 | tf_op jit(solution)/shard_map/all_to_all | solution.py:300
  51.0 0.6 dynamic-slice_bitcast_fusion
  51.6 10.6 %all-to-all-done = bf16[8,8,4096]{2,1,0:T(8,128)(2,1)S(1)} async-done(((bf16[8,8,4096]{2,1,0:T(8,128)(2,1)}), bf16[8,8,4096]{2,1,0:T(8,128)(2,1)S(1)}, u32[]{:S(2)}, u32[]{:S(2)}) %all-to-all-start) | async-done | bytes 524320 | tf_op jit(solution)/shard_map/all_to_all | solution.py:300
  62.2 0.1 convert_reduce_fusion
  62.3 0.7 %copy.27 = f32[1,8,32,128]{3,2,1,0:T(8,128)} copy(f32[1,8,32,128]{3,1,2,0:T(8,128)S(1)} %bitcast.16) | data formatting | bytes 262144
  (7 shorter events, 0.1 us)
Async XLA Ops:
  0.6 0.9 %copy-start = (s32[2048]{0:T(1024)S(1)}, s32[2048]{0:T(1024)}, u32[]{:S(2)}) copy-start(s32[2048]{0:T(1024)} %param.7) | copy-start | bytes 24580
  0.6 2.1 %copy-start.2 = (s32[8]{0:T(128)S(1)}, s32[8]{0:T(128)}, u32[]{:S(2)}) copy-start(s32[8]{0:T(128)} %param.9) | copy-start | bytes 100
  0.7 2.2 %copy-start.1 = (bf16[8,32,128]{2,1,0:T(8,128)(2,1)S(1)}, bf16[8,32,128]{2,1,0:T(8,128)(2,1)}, u32[]{:S(2)}) copy-start(bf16[8,32,128]{2,1,0:T(8,128)(2,1)} %q_ref.1) | copy-start | bytes 196612
  45.6 16.6 %all-to-all-start = ((bf16[8,8,4096]{2,1,0:T(8,128)(2,1)}), bf16[8,8,4096]{2,1,0:T(8,128)(2,1)S(1)}, u32[]{:S(2)}, u32[]{:S(2)}) async-start(bf16[8,8,4096]{2,1,0:T(8,128)(2,1)} %fusion), calls=%async_computation | async-start | bytes 1048576 | tf_op jit(solution)/shard_map/all_to_all | solution.py:300

commit v2 on v1

--- a/solution.py
+++ b/solution.py
@@ -7,7 +7,7 @@
 from jax.experimental.pallas import tpu as pltpu
 from jax.sharding import PartitionSpec as P
 
-GROUP = 64
+GROUP = 96
 
 
 MESH = pl.DeviceIdType.MESH

time: 63.8 us -> 63.4 us (level)
  no operation moved by 1% of the time
where the time goes in v2:
time: 63.4 us; the launch traced here: 63 us
  Pallas kernels  39.3 us (62%)
  waiting for transfers between devices  10.6 us (17%)
  starting transfers between devices  5.33 us (8%)
  local copies, waits for them, and re-layouts  3.37 us (5%)
  matrix products  1.94 us (3%)
  other arithmetic  1.84 us (3%)
  between operations  0.75 us (1%)
    pallas_call x1, Pallas kernels, pair_terms(): pl.pallas_call(pair_kernel, out_shape=(jax.ShapeDtypeStruct((slots, query...  16.1 us
    pallas_call x1, Pallas kernels, gather_queries(): pl.pallas_call(functools.partial(gather_kernel, shards, inner), out_shape...  15.9 us
    all_to_all x1, waiting for transfers between devices, body(): lax.all_to_all(part.reshape(shards, query_rows, query_len * feature_dim),...  10.6 us
    pallas_call x1, Pallas kernels, contrast(): pl.pallas_call(functools.partial(contrast_kernel, shards), out_shape=(jax...  7.17 us
    all_to_all x1, starting transfers between devices, body(): lax.all_to_all(part.reshape(shards, query_rows, query_len * feature_dim),...  5.33 us
    dot_general x1, matrix products, body(): lax.dot_general(coefficients[:, :group], basis.reshape(capacity, query_le...  1.94 us
  transfers between devices with their start and end apart: 1, of which 1 were waited for; matrix products, arithmetic and copies ran while one was open for 1% of the time, Pallas kernels for 0%

profile of v2, /device:TPU:0, one launch (start us, length us, event | category | flops | bytes accessed | tf_op | source)
XLA Modules:
  0.0 63.0 jit_solution(15326605379751266781)
XLA Ops:
  0.6 0.0 copy-start
  0.6 0.0 copy-start.2
  0.7 0.0 copy-start.1
  0.7 0.7 %compare_select_fusion = s32[8,16]{1,0:T(8,128)S(1)} fusion(s32[8,16]{1,0:T(8,128)} %param.8), kind=kLoop, calls=%fused_computation.37 | loop fusion | flops 384 | bytes 1024 | tf_op jit(solution)/shard_map/select_n | solution.py:286
  1.4 0.1 reshape.161
  1.5 0.0 copy-done
  1.5 1.1 %gather_fusion = s32[128]{0:T(128)S(1)} fusion(s32[2048]{0:T(1024)S(1)} %copy-done, s32[1024]{0:T(1024)S(1)} %pad_clamp_fusion), kind=kCustom, calls=%fused_computation | custom fusion | bytes 1536 | tf_op jit(solution)/shard_map/gather | solution.py:286
  2.6 0.1 reshape.160
  2.7 0.0 copy-done.2
  2.7 0.1 copy.14
  2.8 0.1 pad_add_fusion
  2.9 0.0 copy-done.1
  2.9 15.9 %shard_map.68 = (bf16[64,32,128]{2,1,0:T(8,128)(2,1)S(1)}, s32[64,128]{1,0:T(8,128)S(1)}) custom-call(bf16[8,32,128]{2,1,0:T(8,128)(2,1)S(1)} %copy-done.1, s32[8,128]{1,0:T(8,128)S(1)} %pad.4.info_ref), custom_call_target="tpu_custom_call" | custom-call | tf_op jit(solution)/shard_map/pallas_call | solution.py:184
  18.8 0.2 slice_reduce_fusion
  19.1 0.1 reshape.153
  19.2 0.1 reshape.157
  19.2 0.3 reduce-window.9
  19.5 0.1 slice.20
  19.6 0.1 slice_reduce_fusion.1
  19.7 0.1 reshape.151
  19.8 0.1 fusion.14
  19.9 0.1 reshape.158
  20.0 0.1 fusion.20
  20.1 0.2 select_reduce_fusion
  20.3 0.2 fusion.7.meta_ref
  20.5 16.1 %shard_map.69 = (bf16[384,32,128]{2,1,0:T(8,128)(2,1)S(1)}, f32[384,128]{1,0:T(8,128)S(1)}) custom-call(s32[384]{0:T(512)S(1)} %get-tuple-element.18.row_ref, s32[384]{0:T(512)S(1)} %get-tuple-element.19.qid_ref, bf16[64,32,128]{2,1,0:T(8,128)(2,1)S(1)} %get-tuple-element.9.queries_ref, bf16[256,128,128]{2,1,0:T(8,128)(2,1)} %passages_ref.1), custom_call_target="tpu_custom_call" | custom-call | tf_op jit(solution)/shard_map/pallas_call | solution.py:93
  36.7 7.2 %shard_map.70 = (bf16[384,128]{1,0:T(8,128)(2,1)S(1)}, f32[8,128]{1,0:T(8,128)S(1)}) custom-call(f32[384,128]{1,0:T(8,128)S(1)} %get-tuple-element.10.sim_ref, s32[384,1]{1,0:T(8,128)S(1)} %fusion.7.meta_ref), custom_call_target="tpu_custom_call" | custom-call | tf_op jit(solution)/shard_map/pallas_call | solution.py:243
  43.9 1.9 %fusion = bf16[8,8,4096]{2,1,0:T(8,128)(2,1)} fusion(bf16[48,8,32,128]{3,2,1,0:T(8,128)(2,1)S(1)} %bitcast.15, bf16[384,128]{1,0:T(8,128)(2,1)S(1)} %get-tuple-element.12), kind=kOutput, calls=%fused_computation.2 | convolution fusion | flops 201588736 | bytes 3768320 | tf_op jit(solution)/shard_map/dot_general | solution.py:294
  45.8 5.3 %all-to-all-start = ((bf16[8,8,4096]{2,1,0:T(8,128)(2,1)}), bf16[8,8,4096]{2,1,0:T(8,128)(2,1)S(1)}, u32[]{:S(2)}, u32[]{:S(2)}) async-start(bf16[8,8,4096]{2,1,0:T(8,128)(2,1)} %fusion), calls=%async_computation | async-start | bytes 1048576 | tf_op jit(solution)/shard_map/all_to_all | solution.py:300
  51.1 0.6 dynamic-slice_bitcast_fusion
  51.7 10.6 %all-to-all-done = bf16[8,8,4096]{2,1,0:T(8,128)(2,1)S(1)} async-done(((bf16[8,8,4096]{2,1,0:T(8,128)(2,1)}), bf16[8,8,4096]{2,1,0:T(8,128)(2,1)S(1)}, u32[]{:S(2)}, u32[]{:S(2)}) %all-to-all-start) | async-done | bytes 524320 | tf_op jit(solution)/shard_map/all_to_all | solution.py:300
  62.3 0.1 convert_reduce_fusion
  62.4 0.7 %copy.27 = f32[1,8,32,128]{3,2,1,0:T(8,128)} copy(f32[1,8,32,128]{3,1,2,0:T(8,128)S(1)} %bitcast.16) | data formatting | bytes 262144
  (7 shorter events, 0.1 us)
Async XLA Ops:
  0.6 0.9 %copy-start = (s32[2048]{0:T(1024)S(1)}, s32[2048]{0:T(1024)}, u32[]{:S(2)}) copy-start(s32[2048]{0:T(1024)} %param.7) | copy-start | bytes 24580
  0.6 2.1 %copy-start.2 = (s32[8]{0:T(128)S(1)}, s32[8]{0:T(128)}, u32[]{:S(2)}) copy-start(s32[8]{0:T(128)} %param.9) | copy-start | bytes 100
  0.7 2.2 %copy-start.1 = (bf16[8,32,128]{2,1,0:T(8,128)(2,1)S(1)}, bf16[8,32,128]{2,1,0:T(8,128)(2,1)}, u32[]{:S(2)}) copy-start(bf16[8,32,128]{2,1,0:T(8,128)(2,1)} %q_ref.1) | copy-start | bytes 196612
  45.8 16.5 %all-to-all-start = ((bf16[8,8,4096]{2,1,0:T(8,128)(2,1)}), bf16[8,8,4096]{2,1,0:T(8,128)(2,1)S(1)}, u32[]{:S(2)}, u32[]{:S(2)}) async-start(bf16[8,8,4096]{2,1,0:T(8,128)(2,1)} %fusion), calls=%async_computation | async-start | bytes 1048576 | tf_op jit(solution)/shard_map/all_to_all | solution.py:300
